TPU v7x, 32 devices: a whole 2x2x4 slice. The times are simulated.
32 devices in a mesh: groups: 2 (over x), segment: 8 (over z, y), slab: 2 (over core).
Axes of the slice: x: 2, y: 2, z: 4, core: 2. Of those that a mesh axis runs over, the one named last changes fastest.
Arguments:
- fields: float32 [8, 3, 16, 16, 16], P('groups', None, 'slab'), parts along dimension 0, may hold values from -6 to 6
- anchors: int32 [8, 3], P('groups'), parts along dimension 0, may hold values from 0 to 4095
- lift_weight: float32 [64, 6], replicated, may hold values from -2.5 to 2.5
- conv_weight: bfloat16 [8, 3, 9, 64, 192], P('segment'), may hold values from -0.03125 to 0.03125
- conv_bias: float32 [8, 3, 64], P('segment'), may hold values from -1.25 to 1.25
- proj_weight: float32 [3, 64], replicated, may hold values from -0.75 to 0.75
Outputs:
- trajectory: float32 [2, 8, 3, 16, 16, 16], P(None, 'groups', None, 'slab', None, 'segment'), parts along dimension 1
There are 2 independent parts, one for each index of `groups`. A program takes and returns all parts, laid end to end along the dimension named above; an argument that names none is the same for every part. Nothing has to cross between parts.
All inputs are finite; a program needn't handle non-finite values.
Results may differ from a plain program's by a relative error of at most 0.028.
Values may be sent and summed in bfloat16 or wider, within the bound.
No kernel may reach another device: no remote copies, remote signals or barrier semaphores. Data moves between devices by JAX's collectives and lax.ppermute only.
A program may use at most 64 MiB of HBM per device.

v0:
```python
import jax
import jax.numpy as jnp
from jax import lax
from jax.sharding import PartitionSpec as P

LAYERS = 3
STEPS = 2
FIELD = 4096


def extended(array, sides, width):
    for axis, dim in sides:
        size, length = (lax.axis_size(axis), array.shape[dim])
        up = [(i, (i + 1) % size) for i in range(size)]
        down = [(j, i) for i, j in up]
        last = lax.slice_in_dim(array, length - width, length, axis=dim)
        leading = lax.slice_in_dim(array, 0, width, axis=dim)
        before = lax.ppermute(last, axis, up)
        after = lax.ppermute(leading, axis, down)
        array = jnp.concatenate([before, array, after], axis=dim)
    return array


def passed_along(value, axis, steps):
    count = lax.axis_size(axis)
    pairs = [(source, (source + steps) % count) for source in range(count)]
    return lax.ppermute(value, axis, pairs)


def roll_plane(values, shift_y, shift_z, z_cells, z_index):
    moved = jnp.roll(values, -shift_y * z_cells, axis=-1)
    amount = -shift_z % z_cells
    if amount == 0:
        return moved
    return jnp.where(
        z_index >= amount,
        jnp.roll(moved, amount, axis=-1),
        jnp.roll(moved, amount - z_cells, axis=-1),
    )


def dilated_conv(activated, layer_weights, dilation, z_cells, z_index):
    out_rows = activated.shape[1] - 2 * dilation
    summed = None
    for tap_y in (-1, 0, 1):
        columns = jnp.concatenate(
            [
                roll_plane(activated, tap_y * dilation, tap_z * dilation, z_cells, z_index)
                for tap_z in (-1, 0, 1)
            ],
            axis=0,
        )
        for tap_x in (-1, 0, 1):
            begin = dilation + tap_x * dilation
            window = lax.slice_in_dim(columns, begin, begin + out_rows, axis=1)
            product = jnp.einsum(
                "oc,cxp->oxp",
                layer_weights[(tap_x + 1) * 3 + tap_y + 1],
                window,
                preferred_element_type=jnp.float32,
            )
            summed = product if summed is None else summed + product
    return summed


def shards(fields, anchors, lift_weight, conv_weight, conv_bias, proj_weight):
    segments = lax.axis_size("segment")
    segment_id = lax.axis_index("segment")
    slab_id = lax.axis_index("slab")
    crop_count, components, slab_rows, y_cells, z_cells = fields.shape
    plane_size = y_cells * z_cells
    weights = conv_weight[0]
    biases = conv_bias[0]
    flat_fields = fields.reshape(crop_count, components, slab_rows, plane_size)
    z_index = jnp.arange(plane_size, dtype=jnp.int32) % z_cells
    row_index = slab_id * slab_rows + jnp.arange(slab_rows, dtype=jnp.int32)
    y_index = jnp.arange(y_cells, dtype=jnp.int32)
    z_range = jnp.arange(z_cells, dtype=jnp.int32)
    turns = STEPS * segments + crop_count

    def wave(position):
        return jnp.sin(2.0 * jnp.pi * (position % FIELD).astype(jnp.float32) / FIELD)

    def lift_field(field, crop_slot):
        anchor = lax.dynamic_index_in_dim(anchors, crop_slot, 0, keepdims=False)
        wave_x = jnp.broadcast_to(wave(anchor[0] + row_index)[:, None], (slab_rows, plane_size))
        wave_y = jnp.broadcast_to(
            jnp.repeat(wave(anchor[1] + y_index), z_cells)[None, :], (slab_rows, plane_size)
        )
        wave_z = jnp.broadcast_to(
            jnp.tile(wave(anchor[2] + z_range), y_cells)[None, :], (slab_rows, plane_size)
        )
        inputs = jnp.concatenate([field, jnp.stack([wave_x, wave_y, wave_z], axis=0)], axis=0)
        return jnp.einsum(
            "oc,cxp->oxp", lift_weight, inputs, precision=lax.Precision.HIGHEST
        ).astype(jnp.bfloat16)

    def project(hidden):
        return jnp.einsum(
            "oc,cxp->oxp", proj_weight, hidden.astype(jnp.float32), precision=lax.Precision.HIGHEST
        )

    def run_section(entry, active):
        state = entry.astype(jnp.float32)
        for layer in range(LAYERS):
            dilation = 2**layer
            activated = jax.nn.silu(state).astype(jnp.bfloat16)
            widened = extended(activated, (("slab", 1),), dilation)

            def apply_layer(current_state, widened=widened, layer=layer, dilation=dilation):
                return (
                    current_state
                    + dilated_conv(widened, weights[layer], dilation, z_cells, z_index)
                    + biases[layer][:, None, None]
                )

            def keep_layer(current_state, widened=widened):
                return current_state

            state = lax.cond(active, apply_layer, keep_layer, state)
        return state.astype(jnp.bfloat16)

    def turn_step(turn, carry):
        hidden, current, record = carry
        offset = turn - segment_id
        roll_step = jnp.floor_divide(offset, segments)
        crop_index = jnp.remainder(offset, segments)
        crop_slot = jnp.minimum(crop_index, crop_count - 1)
        is_first = segment_id == 0
        arrived = is_first & (roll_step >= 1) & (crop_index < crop_count)
        previous = lax.dynamic_index_in_dim(current, crop_slot, 0, keepdims=False)
        renewed = previous + project(hidden)
        updated = jnp.where(arrived, renewed, previous)
        current = lax.dynamic_update_index_in_dim(current, updated, crop_slot, 0)
        record_step = jnp.clip(roll_step - 1, 0, STEPS - 1)
        placed = lax.dynamic_update_slice(
            record, updated[None, None], (record_step, crop_slot, 0, 0, 0)
        )
        record = jnp.where(arrived, placed, record)
        active = (offset >= 0) & (crop_index < crop_count) & (roll_step < STEPS)
        entry = jnp.where(is_first, lift_field(updated, crop_slot), hidden)
        leaving = run_section(entry, active)
        hidden = passed_along(leaving, "segment", 1)
        return (hidden, current, record)

    hidden = jnp.zeros((conv_weight.shape[3], slab_rows, plane_size), jnp.bfloat16)
    record = jnp.zeros((STEPS, crop_count, components, slab_rows, plane_size), jnp.float32)
    hidden, current, record = lax.fori_loop(0, turns, turn_step, (hidden, flat_fields, record))
    shaped = record.reshape(STEPS, crop_count, components, slab_rows, y_cells, z_cells)
    return lax.psum_scatter(
        shaped.astype(jnp.bfloat16), "segment", scatter_dimension=5, tiled=True
    ).astype(jnp.float32)


def solution(mesh):
    in_specs = (
        P("groups", None, "slab", None, None),
        P("groups", None),
        P(),
        P("segment", None, None, None, None),
        P("segment", None, None),
        P(),
    )
    out_specs = P(None, "groups", None, "slab", None, "segment")
    return jax.shard_map(shards, mesh=mesh, in_specs=in_specs, out_specs=out_specs, check_vma=False)
```

profile of v0, /device:TPU:0, one launch (start us, length us, event | category | flops | bytes accessed | tf_op | source)
XLA Modules:
  0.0 961.1 jit_solution(36993876681847843)
XLA Ops:
  8.8 879.8 %while.23 = (s32[]{:T(128)}, bf16[64,8,256]{2,0,1:T(8,128)(2,1)S(1)}, f32[4,3,8,256]{3,1,2,0:T(4,128)S(1)}, bf16[2,4,3,8,256]{4,2,3,1,0:T(4,128)(2,1)S(1)}, s32[...) while((s32[]{:T(128)}, ...), condition=%wide.region_7.8_spmd.clone.clone, body=%wide.region_0.7_spmd.clone.clone.sunk | while | flops 1472411264 | bytes 135911120 | solution.py:148
  25.5 8.0 conditional.13
  35.5 10.0 %conditional.14 = (f32[64,8,256]{2,0,1:T(8,128)S(1)}) conditional(s32[]{:T(128)} %convert_element_type.196, f32[64,8,256]{2,0,1:T(8,128)S(1)} %get-tuple-element.1073, (s32[256]{0:T(256)S(1)}, s32[256]{0:T(256)S(1)}, s32[256]{0:T(256)S(1)}, bf16[64,16,256]{2,0,1:T(8,128)(2,1)S(1)}, s32[256]{0:T(256)S(1)}, /*index=5*/s32[256]{0:T(256)S(1)}, ...), branch_computations={%region_5.5_spmd, %region_6.6_spmd} | conditional | flops 492865024 | bytes 47392776 | solution.py:120
  45.6 11.1 %collective-permute-done.6 = bf16[64,8,256]{2,0,1:T(8,128)(2,1)S(1)} collective-permute-done((bf16[64,8,256]{2,0,1:T(8,128)(2,1)S(1)}, bf16[64,8,256]{2,0,1:T(8,128)(2,1)S(1)}, u32[]{:S(2)}, u32[]{:S(2)}) %collective-permute-start.6) | collective-permute-done | bytes 262176 | tf_op jit(solution)/shard_map/while/body/eval_jaxpr/ppermute | solution.py:27
  83.0 10.0 %conditional.14 = (f32[64,8,256]{2,0,1:T(8,128)S(1)}) conditional(s32[]{:T(128)} %convert_element_type.196, f32[64,8,256]{2,0,1:T(8,128)S(1)} %get-tuple-element.1073, (s32[256]{0:T(256)S(1)}, s32[256]{0:T(256)S(1)}, s32[256]{0:T(256)S(1)}, bf16[64,16,256]{2,0,1:T(8,128)(2,1)S(1)}, s32[256]{0:T(256)S(1)}, /*index=5*/s32[256]{0:T(256)S(1)}, ...), branch_computations={%region_5.5_spmd, %region_6.6_spmd} | conditional | flops 492865024 | bytes 47392776 | solution.py:120
  93.2 11.2 %collective-permute-done.6 = bf16[64,8,256]{2,0,1:T(8,128)(2,1)S(1)} collective-permute-done((bf16[64,8,256]{2,0,1:T(8,128)(2,1)S(1)}, bf16[64,8,256]{2,0,1:T(8,128)(2,1)S(1)}, u32[]{:S(2)}, u32[]{:S(2)}) %collective-permute-start.6) | collective-permute-done | bytes 262176 | tf_op jit(solution)/shard_map/while/body/eval_jaxpr/ppermute | solution.py:27
  130.7 10.0 %conditional.14 = (f32[64,8,256]{2,0,1:T(8,128)S(1)}) conditional(s32[]{:T(128)} %convert_element_type.196, f32[64,8,256]{2,0,1:T(8,128)S(1)} %get-tuple-element.1073, (s32[256]{0:T(256)S(1)}, s32[256]{0:T(256)S(1)}, s32[256]{0:T(256)S(1)}, bf16[64,16,256]{2,0,1:T(8,128)(2,1)S(1)}, s32[256]{0:T(256)S(1)}, /*index=5*/s32[256]{0:T(256)S(1)}, ...), branch_computations={%region_5.5_spmd, %region_6.6_spmd} | conditional | flops 492865024 | bytes 47392776 | solution.py:120
  140.9 11.2 %collective-permute-done.6 = bf16[64,8,256]{2,0,1:T(8,128)(2,1)S(1)} collective-permute-done((bf16[64,8,256]{2,0,1:T(8,128)(2,1)S(1)}, bf16[64,8,256]{2,0,1:T(8,128)(2,1)S(1)}, u32[]{:S(2)}, u32[]{:S(2)}) %collective-permute-start.6) | collective-permute-done | bytes 262176 | tf_op jit(solution)/shard_map/while/body/eval_jaxpr/ppermute | solution.py:27
  178.4 10.0 %conditional.14 = (f32[64,8,256]{2,0,1:T(8,128)S(1)}) conditional(s32[]{:T(128)} %convert_element_type.196, f32[64,8,256]{2,0,1:T(8,128)S(1)} %get-tuple-element.1073, (s32[256]{0:T(256)S(1)}, s32[256]{0:T(256)S(1)}, s32[256]{0:T(256)S(1)}, bf16[64,16,256]{2,0,1:T(8,128)(2,1)S(1)}, s32[256]{0:T(256)S(1)}, /*index=5*/s32[256]{0:T(256)S(1)}, ...), branch_computations={%region_5.5_spmd, %region_6.6_spmd} | conditional | flops 492865024 | bytes 47392776 | solution.py:120
  188.6 11.2 %collective-permute-done.6 = bf16[64,8,256]{2,0,1:T(8,128)(2,1)S(1)} collective-permute-done((bf16[64,8,256]{2,0,1:T(8,128)(2,1)S(1)}, bf16[64,8,256]{2,0,1:T(8,128)(2,1)S(1)}, u32[]{:S(2)}, u32[]{:S(2)}) %collective-permute-start.6) | collective-permute-done | bytes 262176 | tf_op jit(solution)/shard_map/while/body/eval_jaxpr/ppermute | solution.py:27
  211.2 22.6 %collective-permute-start.6 = (bf16[64,8,256]{2,0,1:T(8,128)(2,1)S(1)}, bf16[64,8,256]{2,0,1:T(8,128)(2,1)S(1)}, u32[]{:S(2)}, u32[]{:S(2)}) collective-permute-start(bf16[64,8,256]{2,0,1:T(8,128)(2,1)S(1)} %convert_element_type.197), channel_id=1, source_target_pairs={{0,2},{2,4},{4,6},{6,8},{8,10},{10,12},{12,14},{14,0},{1,3},{3,5},... | collective-permute-start | bytes 786440 | tf_op jit(solution)/shard_map/while/body/eval_jaxpr/ppermute | solution.py:27
  253.9 8.7 collective-permute-done.6
  274.0 23.5 %collective-permute-start.6 = (bf16[64,8,256]{2,0,1:T(8,128)(2,1)S(1)}, bf16[64,8,256]{2,0,1:T(8,128)(2,1)S(1)}, u32[]{:S(2)}, u32[]{:S(2)}) collective-permute-start(bf16[64,8,256]{2,0,1:T(8,128)(2,1)S(1)} %convert_element_type.197), channel_id=1, source_target_pairs={{0,2},{2,4},{4,6},{6,8},{8,10},{10,12},{12,14},{14,0},{1,3},{3,5},... | collective-permute-start | bytes 786440 | tf_op jit(solution)/shard_map/while/body/eval_jaxpr/ppermute | solution.py:27
  318.5 47.4 %collective-permute-done.6 = bf16[64,8,256]{2,0,1:T(8,128)(2,1)S(1)} collective-permute-done((bf16[64,8,256]{2,0,1:T(8,128)(2,1)S(1)}, bf16[64,8,256]{2,0,1:T(8,128)(2,1)S(1)}, u32[]{:S(2)}, u32[]{:S(2)}) %collective-permute-start.6) | collective-permute-done | bytes 262176 | tf_op jit(solution)/shard_map/while/body/eval_jaxpr/ppermute | solution.py:27
  382.4 8.0 conditional.13
  392.2 10.0 %conditional.14 = (f32[64,8,256]{2,0,1:T(8,128)S(1)}) conditional(s32[]{:T(128)} %convert_element_type.196, f32[64,8,256]{2,0,1:T(8,128)S(1)} %get-tuple-element.1073, (s32[256]{0:T(256)S(1)}, s32[256]{0:T(256)S(1)}, s32[256]{0:T(256)S(1)}, bf16[64,16,256]{2,0,1:T(8,128)(2,1)S(1)}, s32[256]{0:T(256)S(1)}, /*index=5*/s32[256]{0:T(256)S(1)}, ...), branch_computations={%region_5.5_spmd, %region_6.6_spmd} | conditional | flops 492865024 | bytes 47392776 | solution.py:120
  402.4 11.2 %collective-permute-done.6 = bf16[64,8,256]{2,0,1:T(8,128)(2,1)S(1)} collective-permute-done((bf16[64,8,256]{2,0,1:T(8,128)(2,1)S(1)}, bf16[64,8,256]{2,0,1:T(8,128)(2,1)S(1)}, u32[]{:S(2)}, u32[]{:S(2)}) %collective-permute-start.6) | collective-permute-done | bytes 262176 | tf_op jit(solution)/shard_map/while/body/eval_jaxpr/ppermute | solution.py:27
  439.9 10.0 %conditional.14 = (f32[64,8,256]{2,0,1:T(8,128)S(1)}) conditional(s32[]{:T(128)} %convert_element_type.196, f32[64,8,256]{2,0,1:T(8,128)S(1)} %get-tuple-element.1073, (s32[256]{0:T(256)S(1)}, s32[256]{0:T(256)S(1)}, s32[256]{0:T(256)S(1)}, bf16[64,16,256]{2,0,1:T(8,128)(2,1)S(1)}, s32[256]{0:T(256)S(1)}, /*index=5*/s32[256]{0:T(256)S(1)}, ...), branch_computations={%region_5.5_spmd, %region_6.6_spmd} | conditional | flops 492865024 | bytes 47392776 | solution.py:120
  450.1 11.2 %collective-permute-done.6 = bf16[64,8,256]{2,0,1:T(8,128)(2,1)S(1)} collective-permute-done((bf16[64,8,256]{2,0,1:T(8,128)(2,1)S(1)}, bf16[64,8,256]{2,0,1:T(8,128)(2,1)S(1)}, u32[]{:S(2)}, u32[]{:S(2)}) %collective-permute-start.6) | collective-permute-done | bytes 262176 | tf_op jit(solution)/shard_map/while/body/eval_jaxpr/ppermute | solution.py:27
  487.6 10.0 %conditional.14 = (f32[64,8,256]{2,0,1:T(8,128)S(1)}) conditional(s32[]{:T(128)} %convert_element_type.196, f32[64,8,256]{2,0,1:T(8,128)S(1)} %get-tuple-element.1073, (s32[256]{0:T(256)S(1)}, s32[256]{0:T(256)S(1)}, s32[256]{0:T(256)S(1)}, bf16[64,16,256]{2,0,1:T(8,128)(2,1)S(1)}, s32[256]{0:T(256)S(1)}, /*index=5*/s32[256]{0:T(256)S(1)}, ...), branch_computations={%region_5.5_spmd, %region_6.6_spmd} | conditional | flops 492865024 | bytes 47392776 | solution.py:120
  497.8 11.2 %collective-permute-done.6 = bf16[64,8,256]{2,0,1:T(8,128)(2,1)S(1)} collective-permute-done((bf16[64,8,256]{2,0,1:T(8,128)(2,1)S(1)}, bf16[64,8,256]{2,0,1:T(8,128)(2,1)S(1)}, u32[]{:S(2)}, u32[]{:S(2)}) %collective-permute-start.6) | collective-permute-done | bytes 262176 | tf_op jit(solution)/shard_map/while/body/eval_jaxpr/ppermute | solution.py:27
  535.3 10.0 %conditional.14 = (f32[64,8,256]{2,0,1:T(8,128)S(1)}) conditional(s32[]{:T(128)} %convert_element_type.196, f32[64,8,256]{2,0,1:T(8,128)S(1)} %get-tuple-element.1073, (s32[256]{0:T(256)S(1)}, s32[256]{0:T(256)S(1)}, s32[256]{0:T(256)S(1)}, bf16[64,16,256]{2,0,1:T(8,128)(2,1)S(1)}, s32[256]{0:T(256)S(1)}, /*index=5*/s32[256]{0:T(256)S(1)}, ...), branch_computations={%region_5.5_spmd, %region_6.6_spmd} | conditional | flops 492865024 | bytes 47392776 | solution.py:120
  545.5 11.2 %collective-permute-done.6 = bf16[64,8,256]{2,0,1:T(8,128)(2,1)S(1)} collective-permute-done((bf16[64,8,256]{2,0,1:T(8,128)(2,1)S(1)}, bf16[64,8,256]{2,0,1:T(8,128)(2,1)S(1)}, u32[]{:S(2)}, u32[]{:S(2)}) %collective-permute-start.6) | collective-permute-done | bytes 262176 | tf_op jit(solution)/shard_map/while/body/eval_jaxpr/ppermute | solution.py:27
  568.1 22.6 %collective-permute-start.6 = (bf16[64,8,256]{2,0,1:T(8,128)(2,1)S(1)}, bf16[64,8,256]{2,0,1:T(8,128)(2,1)S(1)}, u32[]{:S(2)}, u32[]{:S(2)}) collective-permute-start(bf16[64,8,256]{2,0,1:T(8,128)(2,1)S(1)} %convert_element_type.197), channel_id=1, source_target_pairs={{0,2},{2,4},{4,6},{6,8},{8,10},{10,12},{12,14},{14,0},{1,3},{3,5},... | collective-permute-start | bytes 786440 | tf_op jit(solution)/shard_map/while/body/eval_jaxpr/ppermute | solution.py:27
  610.8 8.7 collective-permute-done.6
  631.0 23.5 %collective-permute-start.6 = (bf16[64,8,256]{2,0,1:T(8,128)(2,1)S(1)}, bf16[64,8,256]{2,0,1:T(8,128)(2,1)S(1)}, u32[]{:S(2)}, u32[]{:S(2)}) collective-permute-start(bf16[64,8,256]{2,0,1:T(8,128)(2,1)S(1)} %convert_element_type.197), channel_id=1, source_target_pairs={{0,2},{2,4},{4,6},{6,8},{8,10},{10,12},{12,14},{14,0},{1,3},{3,5},... | collective-permute-start | bytes 786440 | tf_op jit(solution)/shard_map/while/body/eval_jaxpr/ppermute | solution.py:27
  675.4 47.4 %collective-permute-done.6 = bf16[64,8,256]{2,0,1:T(8,128)(2,1)S(1)} collective-permute-done((bf16[64,8,256]{2,0,1:T(8,128)(2,1)S(1)}, bf16[64,8,256]{2,0,1:T(8,128)(2,1)S(1)}, u32[]{:S(2)}, u32[]{:S(2)}) %collective-permute-start.6) | collective-permute-done | bytes 262176 | tf_op jit(solution)/shard_map/while/body/eval_jaxpr/ppermute | solution.py:27
  734.3 36.2 %collective-permute-done.6 = bf16[64,8,256]{2,0,1:T(8,128)(2,1)S(1)} collective-permute-done((bf16[64,8,256]{2,0,1:T(8,128)(2,1)S(1)}, bf16[64,8,256]{2,0,1:T(8,128)(2,1)S(1)}, u32[]{:S(2)}, u32[]{:S(2)}) %collective-permute-start.6) | collective-permute-done | bytes 262176 | tf_op jit(solution)/shard_map/while/body/eval_jaxpr/ppermute | solution.py:27
  782.0 36.2 %collective-permute-done.6 = bf16[64,8,256]{2,0,1:T(8,128)(2,1)S(1)} collective-permute-done((bf16[64,8,256]{2,0,1:T(8,128)(2,1)S(1)}, bf16[64,8,256]{2,0,1:T(8,128)(2,1)S(1)}, u32[]{:S(2)}, u32[]{:S(2)}) %collective-permute-start.6) | collective-permute-done | bytes 262176 | tf_op jit(solution)/shard_map/while/body/eval_jaxpr/ppermute | solution.py:27
  829.7 36.2 %collective-permute-done.6 = bf16[64,8,256]{2,0,1:T(8,128)(2,1)S(1)} collective-permute-done((bf16[64,8,256]{2,0,1:T(8,128)(2,1)S(1)}, bf16[64,8,256]{2,0,1:T(8,128)(2,1)S(1)}, u32[]{:S(2)}, u32[]{:S(2)}) %collective-permute-start.6) | collective-permute-done | bytes 262176 | tf_op jit(solution)/shard_map/while/body/eval_jaxpr/ppermute | solution.py:27
  877.4 11.2 %collective-permute-done.6 = bf16[64,8,256]{2,0,1:T(8,128)(2,1)S(1)} collective-permute-done((bf16[64,8,256]{2,0,1:T(8,128)(2,1)S(1)}, bf16[64,8,256]{2,0,1:T(8,128)(2,1)S(1)}, u32[]{:S(2)}, u32[]{:S(2)}) %collective-permute-start.6) | collective-permute-done | bytes 262176 | tf_op jit(solution)/shard_map/while/body/eval_jaxpr/ppermute | solution.py:27
  891.3 61.2 %reduce-scatter.2.cloned.1.call-done = bf16[2,4,3,8,16,2]{4,3,2,1,0,5:T(8,128)(2,1)} async-done(((bf16[2,4,3,8,16,16]{4,3,2,1,0,5:T(8,128)(2,1)}), bf16[2,4,3,8,16,2]{4,3,2,1,0,5:T(8,128)(2,1)}) %reduce-scatter.2.cloned.1.call-update) | async-done | bytes 12304 | tf_op jit(solution)/shard_map/reduce_scatter | solution.py:150
  (1560 shorter events, 568.3 us)
Async XLA Ops:
  6.5 946.0 %reduce-scatter.2.cloned.1.call-start = ((), (), s32[]{:S(2)}) async-start(), calls=%async_computation.1 | async-start | bytes 884736 | tf_op jit(solution)/shard_map/reduce_scatter | solution.py:150
  33.6 1.4 collective-permute-start.4
  45.5 11.1 %collective-permute-start.6 = (bf16[64,8,256]{2,0,1:T(8,128)(2,1)S(1)}, bf16[64,8,256]{2,0,1:T(8,128)(2,1)S(1)}, u32[]{:S(2)}, u32[]{:S(2)}) collective-permute-start(bf16[64,8,256]{2,0,1:T(8,128)(2,1)S(1)} %convert_element_type.197), channel_id=1, source_target_pairs={{0,2},{2,4},{4,6},{6,8},{8,10},{10,12},{12,14},{14,0},{1,3},{3,5},... | collective-permute-start | bytes 786440 | tf_op jit(solution)/shard_map/while/body/eval_jaxpr/ppermute | solution.py:27
  81.3 1.4 collective-permute-start.4
  93.1 11.3 %collective-permute-start.6 = (bf16[64,8,256]{2,0,1:T(8,128)(2,1)S(1)}, bf16[64,8,256]{2,0,1:T(8,128)(2,1)S(1)}, u32[]{:S(2)}, u32[]{:S(2)}) collective-permute-start(bf16[64,8,256]{2,0,1:T(8,128)(2,1)S(1)} %convert_element_type.197), channel_id=1, source_target_pairs={{0,2},{2,4},{4,6},{6,8},{8,10},{10,12},{12,14},{14,0},{1,3},{3,5},... | collective-permute-start | bytes 786440 | tf_op jit(solution)/shard_map/while/body/eval_jaxpr/ppermute | solution.py:27
  129.0 1.4 collective-permute-start.4
  140.8 11.3 %collective-permute-start.6 = (bf16[64,8,256]{2,0,1:T(8,128)(2,1)S(1)}, bf16[64,8,256]{2,0,1:T(8,128)(2,1)S(1)}, u32[]{:S(2)}, u32[]{:S(2)}) collective-permute-start(bf16[64,8,256]{2,0,1:T(8,128)(2,1)S(1)} %convert_element_type.197), channel_id=1, source_target_pairs={{0,2},{2,4},{4,6},{6,8},{8,10},{10,12},{12,14},{14,0},{1,3},{3,5},... | collective-permute-start | bytes 786440 | tf_op jit(solution)/shard_map/while/body/eval_jaxpr/ppermute | solution.py:27
  176.7 1.4 collective-permute-start.4
  188.5 11.3 %collective-permute-start.6 = (bf16[64,8,256]{2,0,1:T(8,128)(2,1)S(1)}, bf16[64,8,256]{2,0,1:T(8,128)(2,1)S(1)}, u32[]{:S(2)}, u32[]{:S(2)}) collective-permute-start(bf16[64,8,256]{2,0,1:T(8,128)(2,1)S(1)} %convert_element_type.197), channel_id=1, source_target_pairs={{0,2},{2,4},{4,6},{6,8},{8,10},{10,12},{12,14},{14,0},{1,3},{3,5},... | collective-permute-start | bytes 786440 | tf_op jit(solution)/shard_map/while/body/eval_jaxpr/ppermute | solution.py:27
  209.5 1.4 collective-permute-start.4
  211.2 28.7 %collective-permute-start.6 = (bf16[64,8,256]{2,0,1:T(8,128)(2,1)S(1)}, bf16[64,8,256]{2,0,1:T(8,128)(2,1)S(1)}, u32[]{:S(2)}, u32[]{:S(2)}) collective-permute-start(bf16[64,8,256]{2,0,1:T(8,128)(2,1)S(1)} %convert_element_type.197), channel_id=1, source_target_pairs={{0,2},{2,4},{4,6},{6,8},{8,10},{10,12},{12,14},{14,0},{1,3},{3,5},... | collective-permute-start | bytes 786440 | tf_op jit(solution)/shard_map/while/body/eval_jaxpr/ppermute | solution.py:27
  249.6 1.4 collective-permute-start.4
  251.3 11.3 %collective-permute-start.6 = (bf16[64,8,256]{2,0,1:T(8,128)(2,1)S(1)}, bf16[64,8,256]{2,0,1:T(8,128)(2,1)S(1)}, u32[]{:S(2)}, u32[]{:S(2)}) collective-permute-start(bf16[64,8,256]{2,0,1:T(8,128)(2,1)S(1)} %convert_element_type.197), channel_id=1, source_target_pairs={{0,2},{2,4},{4,6},{6,8},{8,10},{10,12},{12,14},{14,0},{1,3},{3,5},... | collective-permute-start | bytes 786440 | tf_op jit(solution)/shard_map/while/body/eval_jaxpr/ppermute | solution.py:27
  272.3 1.4 collective-permute-start.4
  274.0 29.6 %collective-permute-start.6 = (bf16[64,8,256]{2,0,1:T(8,128)(2,1)S(1)}, bf16[64,8,256]{2,0,1:T(8,128)(2,1)S(1)}, u32[]{:S(2)}, u32[]{:S(2)}) collective-permute-start(bf16[64,8,256]{2,0,1:T(8,128)(2,1)S(1)} %convert_element_type.197), channel_id=1, source_target_pairs={{0,2},{2,4},{4,6},{6,8},{8,10},{10,12},{12,14},{14,0},{1,3},{3,5},... | collective-permute-start | bytes 786440 | tf_op jit(solution)/shard_map/while/body/eval_jaxpr/ppermute | solution.py:27
  313.3 1.4 collective-permute-start.4
  315.0 50.8 %collective-permute-start.6 = (bf16[64,8,256]{2,0,1:T(8,128)(2,1)S(1)}, bf16[64,8,256]{2,0,1:T(8,128)(2,1)S(1)}, u32[]{:S(2)}, u32[]{:S(2)}) collective-permute-start(bf16[64,8,256]{2,0,1:T(8,128)(2,1)S(1)} %convert_element_type.197), channel_id=1, source_target_pairs={{0,2},{2,4},{4,6},{6,8},{8,10},{10,12},{12,14},{14,0},{1,3},{3,5},... | collective-permute-start | bytes 786440 | tf_op jit(solution)/shard_map/while/body/eval_jaxpr/ppermute | solution.py:27
  390.6 1.4 collective-permute-start.4
  402.3 11.3 %collective-permute-start.6 = (bf16[64,8,256]{2,0,1:T(8,128)(2,1)S(1)}, bf16[64,8,256]{2,0,1:T(8,128)(2,1)S(1)}, u32[]{:S(2)}, u32[]{:S(2)}) collective-permute-start(bf16[64,8,256]{2,0,1:T(8,128)(2,1)S(1)} %convert_element_type.197), channel_id=1, source_target_pairs={{0,2},{2,4},{4,6},{6,8},{8,10},{10,12},{12,14},{14,0},{1,3},{3,5},... | collective-permute-start | bytes 786440 | tf_op jit(solution)/shard_map/while/body/eval_jaxpr/ppermute | solution.py:27
  450.0 11.3 %collective-permute-start.6 = (bf16[64,8,256]{2,0,1:T(8,128)(2,1)S(1)}, bf16[64,8,256]{2,0,1:T(8,128)(2,1)S(1)}, u32[]{:S(2)}, u32[]{:S(2)}) collective-permute-start(bf16[64,8,256]{2,0,1:T(8,128)(2,1)S(1)} %convert_element_type.197), channel_id=1, source_target_pairs={{0,2},{2,4},{4,6},{6,8},{8,10},{10,12},{12,14},{14,0},{1,3},{3,5},... | collective-permute-start | bytes 786440 | tf_op jit(solution)/shard_map/while/body/eval_jaxpr/ppermute | solution.py:27
  497.7 11.3 %collective-permute-start.6 = (bf16[64,8,256]{2,0,1:T(8,128)(2,1)S(1)}, bf16[64,8,256]{2,0,1:T(8,128)(2,1)S(1)}, u32[]{:S(2)}, u32[]{:S(2)}) collective-permute-start(bf16[64,8,256]{2,0,1:T(8,128)(2,1)S(1)} %convert_element_type.197), channel_id=1, source_target_pairs={{0,2},{2,4},{4,6},{6,8},{8,10},{10,12},{12,14},{14,0},{1,3},{3,5},... | collective-permute-start | bytes 786440 | tf_op jit(solution)/shard_map/while/body/eval_jaxpr/ppermute | solution.py:27
  545.4 11.3 %collective-permute-start.6 = (bf16[64,8,256]{2,0,1:T(8,128)(2,1)S(1)}, bf16[64,8,256]{2,0,1:T(8,128)(2,1)S(1)}, u32[]{:S(2)}, u32[]{:S(2)}) collective-permute-start(bf16[64,8,256]{2,0,1:T(8,128)(2,1)S(1)} %convert_element_type.197), channel_id=1, source_target_pairs={{0,2},{2,4},{4,6},{6,8},{8,10},{10,12},{12,14},{14,0},{1,3},{3,5},... | collective-permute-start | bytes 786440 | tf_op jit(solution)/shard_map/while/body/eval_jaxpr/ppermute | solution.py:27
  568.1 28.7 %collective-permute-start.6 = (bf16[64,8,256]{2,0,1:T(8,128)(2,1)S(1)}, bf16[64,8,256]{2,0,1:T(8,128)(2,1)S(1)}, u32[]{:S(2)}, u32[]{:S(2)}) collective-permute-start(bf16[64,8,256]{2,0,1:T(8,128)(2,1)S(1)} %convert_element_type.197), channel_id=1, source_target_pairs={{0,2},{2,4},{4,6},{6,8},{8,10},{10,12},{12,14},{14,0},{1,3},{3,5},... | collective-permute-start | bytes 786440 | tf_op jit(solution)/shard_map/while/body/eval_jaxpr/ppermute | solution.py:27
  608.2 11.3 %collective-permute-start.6 = (bf16[64,8,256]{2,0,1:T(8,128)(2,1)S(1)}, bf16[64,8,256]{2,0,1:T(8,128)(2,1)S(1)}, u32[]{:S(2)}, u32[]{:S(2)}) collective-permute-start(bf16[64,8,256]{2,0,1:T(8,128)(2,1)S(1)} %convert_element_type.197), channel_id=1, source_target_pairs={{0,2},{2,4},{4,6},{6,8},{8,10},{10,12},{12,14},{14,0},{1,3},{3,5},... | collective-permute-start | bytes 786440 | tf_op jit(solution)/shard_map/while/body/eval_jaxpr/ppermute | solution.py:27
  631.0 29.6 %collective-permute-start.6 = (bf16[64,8,256]{2,0,1:T(8,128)(2,1)S(1)}, bf16[64,8,256]{2,0,1:T(8,128)(2,1)S(1)}, u32[]{:S(2)}, u32[]{:S(2)}) collective-permute-start(bf16[64,8,256]{2,0,1:T(8,128)(2,1)S(1)} %convert_element_type.197), channel_id=1, source_target_pairs={{0,2},{2,4},{4,6},{6,8},{8,10},{10,12},{12,14},{14,0},{1,3},{3,5},... | collective-permute-start | bytes 786440 | tf_op jit(solution)/shard_map/while/body/eval_jaxpr/ppermute | solution.py:27
  670.3 1.4 collective-permute-start.4
  672.0 50.8 %collective-permute-start.6 = (bf16[64,8,256]{2,0,1:T(8,128)(2,1)S(1)}, bf16[64,8,256]{2,0,1:T(8,128)(2,1)S(1)}, u32[]{:S(2)}, u32[]{:S(2)}) collective-permute-start(bf16[64,8,256]{2,0,1:T(8,128)(2,1)S(1)} %convert_element_type.197), channel_id=1, source_target_pairs={{0,2},{2,4},{4,6},{6,8},{8,10},{10,12},{12,14},{14,0},{1,3},{3,5},... | collective-permute-start | bytes 786440 | tf_op jit(solution)/shard_map/while/body/eval_jaxpr/ppermute | solution.py:27
  734.2 36.3 %collective-permute-start.6 = (bf16[64,8,256]{2,0,1:T(8,128)(2,1)S(1)}, bf16[64,8,256]{2,0,1:T(8,128)(2,1)S(1)}, u32[]{:S(2)}, u32[]{:S(2)}) collective-permute-start(bf16[64,8,256]{2,0,1:T(8,128)(2,1)S(1)} %convert_element_type.197), channel_id=1, source_target_pairs={{0,2},{2,4},{4,6},{6,8},{8,10},{10,12},{12,14},{14,0},{1,3},{3,5},... | collective-permute-start | bytes 786440 | tf_op jit(solution)/shard_map/while/body/eval_jaxpr/ppermute | solution.py:27
  781.9 36.3 %collective-permute-start.6 = (bf16[64,8,256]{2,0,1:T(8,128)(2,1)S(1)}, bf16[64,8,256]{2,0,1:T(8,128)(2,1)S(1)}, u32[]{:S(2)}, u32[]{:S(2)}) collective-permute-start(bf16[64,8,256]{2,0,1:T(8,128)(2,1)S(1)} %convert_element_type.197), channel_id=1, source_target_pairs={{0,2},{2,4},{4,6},{6,8},{8,10},{10,12},{12,14},{14,0},{1,3},{3,5},... | collective-permute-start | bytes 786440 | tf_op jit(solution)/shard_map/while/body/eval_jaxpr/ppermute | solution.py:27
  827.9 1.4 collective-permute-start.4
  829.6 36.3 %collective-permute-start.6 = (bf16[64,8,256]{2,0,1:T(8,128)(2,1)S(1)}, bf16[64,8,256]{2,0,1:T(8,128)(2,1)S(1)}, u32[]{:S(2)}, u32[]{:S(2)}) collective-permute-start(bf16[64,8,256]{2,0,1:T(8,128)(2,1)S(1)} %convert_element_type.197), channel_id=1, source_target_pairs={{0,2},{2,4},{4,6},{6,8},{8,10},{10,12},{12,14},{14,0},{1,3},{3,5},... | collective-permute-start | bytes 786440 | tf_op jit(solution)/shard_map/while/body/eval_jaxpr/ppermute | solution.py:27
  877.3 11.3 %collective-permute-start.6 = (bf16[64,8,256]{2,0,1:T(8,128)(2,1)S(1)}, bf16[64,8,256]{2,0,1:T(8,128)(2,1)S(1)}, u32[]{:S(2)}, u32[]{:S(2)}) collective-permute-start(bf16[64,8,256]{2,0,1:T(8,128)(2,1)S(1)} %convert_element_type.197), channel_id=1, source_target_pairs={{0,2},{2,4},{4,6},{6,8},{8,10},{10,12},{12,14},{14,0},{1,3},{3,5},... | collective-permute-start | bytes 786440 | tf_op jit(solution)/shard_map/while/body/eval_jaxpr/ppermute | solution.py:27
  (129 other events, 204.8 us)
Sparse Core Ops, SparseCore 0:
  891.5 61.0 reduce-scatter.1
where the time goes:
time: 964 us; the launch traced here: 961 us
  waiting for transfers between devices  466 us (48%)
  other arithmetic  152 us (16%)
  starting transfers between devices  139 us (14%)
  matrix products  105 us (11%)
  local copies, waits for them, and re-layouts  76 us (8%)
  between operations  13.4 us (1%)
    ppermute x20, waiting for transfers between devices, passed_along(): return lax.ppermute(value, axis, pairs)  346 us
    ppermute x20, starting transfers between devices, passed_along(): return lax.ppermute(value, axis, pairs)  105 us
    select_n x144, other arithmetic, roll_plane(): jnp.where(z_index >= amount, jnp.roll(moved, amount, axis=-1), jnp.roll(m...  62.8 us
    reduce_scatter x1, waiting for transfers between devices, shards(): lax.psum_scatter(shaped.astype(jnp.bfloat16), 'segment', scatter_dimensio...  61.2 us
    dot_general x216, matrix products, dilated_conv(): jnp.einsum('oc,cxp->oxp', layer_weights[(tap_x + 1) * 3 + tap_y + 1], win...  57.1 us
    ppermute x60, waiting for transfers between devices, extended(): after = lax.ppermute(leading, axis, down)  45.6 us
    sin x40, other arithmetic, wave(): jnp.sin(2.0 * jnp.pi * (position % FIELD).astype(jnp.float32) / FIELD)  39.4 us
    dot_general x20, matrix products, lift_field(): jnp.einsum('oc,cxp->oxp', lift_weight, inputs, precision=lax.Precision.HI...  30 us
  transfers between devices with their start and end apart: 141, of which 141 were waited for; matrix products, arithmetic and copies ran while one was open for 0% of the time, Pallas kernels for 0%

commit v1 on v0

v1 whole, which is shorter than its diff:
```python
import jax
import jax.numpy as jnp
from jax import lax
from jax.experimental import pallas as pl
from jax.experimental.pallas import tpu as pltpu
from jax.sharding import PartitionSpec as P

STEPS = 2
FIELD = 4096
LAYERS = 3
CH = 64
ROWS = 960
VMEM_BYTES = 48 * 1024 * 1024

MOVES = (
    [(4 * b + m, 4 * b + 2 + m, 4 * m + b, 4 * m + 2 + b) for m in range(2) for b in range(2)],
    [(2 * m, 2 * m + 1, m, 4 + m) for m in range(4)],
    [(4 * p + 2 * m, 4 * p + 2 * m + 1, 2 * p + m, 2 * (2 + p) + m) for p in range(2) for m in range(2)],
)
NEXT = (
    [(k + 1) % 8 for k in range(8)],
    [4 * (k // 4) + (k % 4 + 1) % 4 for k in range(8)],
    [2 * (k // 2) + (k % 2 + 1) % 2 for k in range(8)],
)


def low_lanes(shape):
    return lax.broadcasted_iota(jnp.int32, shape, len(shape) - 1) < CH


def nt_dot(a, b):
    return lax.dot_general(a, b, (((1,), (1,)), ((), ())), preferred_element_type=jnp.float32)


def pack_kernel(raw_ref, eye_ref, out_ref):
    eye = eye_ref[...]
    for layer in range(LAYERS):
        for ty in range(3):
            pair = jnp.concatenate([raw_ref[layer, 3 + ty], raw_ref[layer, ty]], axis=0)
            out_ref[layer, ty * 192 : (ty + 1) * 192, :] = nt_dot(eye, pair).astype(jnp.bfloat16)
        pair = jnp.concatenate([raw_ref[layer, 6], raw_ref[layer, 7]], axis=0)
        out_ref[layer, 576:768, :] = nt_dot(eye, pair).astype(jnp.bfloat16)
        pair = jnp.concatenate([raw_ref[layer, 8], raw_ref[layer, 8]], axis=0)
        out_ref[layer, 768:960, :] = nt_dot(eye, pair).astype(jnp.bfloat16)


def expand(packed_ref, section, layer, w_ref):
    low = low_lanes((192, 128))
    zero = jnp.zeros((192, 128), jnp.float32)
    for ty in range(3):
        mid = packed_ref[section, layer, ty * 192 : (ty + 1) * 192, :].astype(jnp.float32)
        rolled = pltpu.roll(mid, CH, 1)
        begin = 576 if ty < 2 else 768
        last = packed_ref[section, layer, begin : begin + 192, :].astype(jnp.float32)
        last_rolled = pltpu.roll(last, CH, 1)
        if ty == 1:
            last, last_rolled = last_rolled, last
        blocks = (
            jnp.where(low, rolled, zero),
            mid,
            jnp.where(low, last, rolled),
            jnp.where(low, zero, last_rolled),
        )
        for a, block in enumerate(blocks):
            block = block.astype(jnp.bfloat16)
            for tz in range(3):
                w_ref[ty * 256 + a * CH : ty * 256 + (a + 1) * CH, tz * 128 : (tz + 1) * 128] = block[
                    tz * CH : (tz + 1) * CH
                ]


def spread(state_in, state_out, f_ref, layer):
    d = 2**layer
    low = low_lanes((16, 16, 128))
    for u_at, v_at, low_at, high_at in MOVES[layer]:
        u = state_in[u_at]
        v = state_in[v_at]
        pairs = (
            (low_at, jnp.where(low, u, pltpu.roll(v, CH, 2))),
            (high_at, jnp.where(low, pltpu.roll(u, CH, 2), v)),
        )
        for at, value in pairs:
            state_out[at] = value
            activated = value * (0.5 * jnp.tanh(0.5 * value) + 0.5)
            turned = pltpu.roll(activated, CH, 2).astype(jnp.bfloat16)
            following = NEXT[layer][at]
            for place, lanes in ((at, slice(CH, 128)), (following, slice(0, CH))):
                part = turned[:, :, lanes]
                f_ref[place, 4:20, :, lanes] = part
                f_ref[place, 4 - d : 4, :, lanes] = part[16 - d :]
                f_ref[place, 20 : 20 + d, :, lanes] = part[:d]


def convolve(state, f_ref, w_ref, bias, layer):
    d = 2**layer
    for k in range(8):
        following = NEXT[layer][k]
        columns = []
        for ty in (-1, 0, 1):
            begin = 4 + d * ty
            columns.append(f_ref[k, begin : begin + 16].reshape(256, 128))
            columns.append(f_ref[following, begin : begin + 16].reshape(256, 128))
        product = jnp.dot(jnp.concatenate(columns, axis=1), w_ref[...], preferred_element_type=jnp.float32)
        product = product.reshape(16, 16, 384)
        total = state[k] + bias + product[:, :, 128:256]
        total = total + pltpu.roll(product[:, :, 0:128], d, 1) + pltpu.roll(product[:, :, 256:384], 16 - d, 1)
        if layer == LAYERS - 1:
            total = total.astype(jnp.bfloat16).astype(jnp.float32)
        state[k] = total


def rollout_kernel(x_ref, lift_ref, proj_ref, packed_ref, bias_ref, out_ref, s_a, s_b, f_ref, w_ref, cur):
    cur[...] = x_ref[...]

    def rollout_step(t, unused):
        x = cur[...]
        high = x.astype(jnp.bfloat16).astype(jnp.float32)
        columns = jnp.concatenate([high, x - high, high], axis=0).T.astype(jnp.bfloat16)
        hidden = jnp.dot(columns, lift_ref[...], preferred_element_type=jnp.float32)
        s_a[...] = hidden.astype(jnp.bfloat16).astype(jnp.float32).reshape(8, 16, 16, 128)

        def section(s, unused):
            states = (s_a, s_b)
            for layer in range(LAYERS):
                before, after = states[layer % 2], states[1 - layer % 2]
                expand(packed_ref, s, layer, w_ref)
                spread(before, after, f_ref, layer)
                convolve(after, f_ref, w_ref, bias_ref[s, layer][None], layer)
            s_a[...] = s_b[...]
            return 0

        lax.fori_loop(0, packed_ref.shape[0], section, 0)
        last = s_a[...].reshape(2048, 128).astype(jnp.bfloat16)
        gain = nt_dot(proj_ref[...], last)
        renewed = cur[...] + gain[:16] + gain[16:32] + gain[32:48]
        cur[...] = renewed
        out_ref[t] = renewed
        return 0

    lax.fori_loop(0, STEPS, rollout_step, 0)


def split_terms(matrix):
    first = matrix.astype(jnp.bfloat16)
    rest = matrix - first.astype(jnp.float32)
    second = rest.astype(jnp.bfloat16)
    third = (rest - second.astype(jnp.float32)).astype(jnp.bfloat16)
    return first, second, third


def shards(fields, anchors, lift_weight, conv_weight, conv_bias, proj_weight):
    segments = lax.axis_size("segment")
    segment_id = lax.axis_index("segment")
    slab_id = lax.axis_index("slab")
    crop_count, comps, slab_rows, y_cells, z_cells = fields.shape
    slot = segment_id % crop_count
    vmem = pl.BlockSpec(memory_space=pltpu.VMEM)

    packed = pl.pallas_call(
        pack_kernel,
        out_shape=jax.ShapeDtypeStruct((LAYERS, ROWS, 128), jnp.bfloat16),
        in_specs=[vmem, vmem],
        out_specs=vmem,
        compiler_params=pltpu.CompilerParams(vmem_limit_bytes=VMEM_BYTES),
    )(conv_weight[0], jnp.eye(192, dtype=jnp.bfloat16))
    packed = lax.all_gather(packed, "segment")
    biases = lax.all_gather(conv_bias[0], "segment")
    biases = jnp.concatenate([biases, biases], axis=2)[:, :, None, :]

    mine = lax.dynamic_index_in_dim(fields, slot, 0, keepdims=False)
    other = lax.ppermute(mine, "slab", [(0, 1), (1, 0)])
    halves = jnp.where(slab_id == 0, jnp.stack([mine, other]), jnp.stack([other, mine]))
    anchor = lax.dynamic_index_in_dim(anchors, slot, 0, keepdims=False)

    def wave(column, length):
        position = (anchor[column] + jnp.arange(length, dtype=jnp.int32)) % FIELD
        return jnp.sin(2.0 * jnp.pi * position.astype(jnp.float32) / FIELD)

    shape = (2, 2, 4, y_cells, z_cells)
    current = halves.reshape(2, comps, 2, 4, y_cells, z_cells).transpose(2, 1, 3, 0, 4, 5).reshape(6, 2048)
    wave_x = jnp.broadcast_to(wave(0, 2 * slab_rows).reshape(2, 2, 4, 1, 1), shape)
    wave_y = jnp.broadcast_to(wave(1, y_cells)[:, None], shape)
    wave_z = jnp.broadcast_to(wave(2, z_cells), shape)
    waves = jnp.stack([wave_x, wave_y, wave_z]).transpose(2, 0, 3, 1, 4, 5).reshape(6, 2048)
    x = jnp.concatenate([current, waves, jnp.zeros((4, 2048), jnp.float32)], axis=0)

    half = jnp.eye(2, dtype=jnp.float32)
    lift_cur = jnp.einsum("ab,of->afbo", half, lift_weight[:, :comps]).reshape(6, 128)
    lift_wave = jnp.einsum("ab,of->afbo", half, lift_weight[:, comps:]).reshape(6, 128)
    lift = jnp.concatenate([lift_cur, lift_wave, jnp.zeros((4, 128), jnp.float32)], axis=0)
    first, second, unused = split_terms(lift)
    lift = jnp.concatenate([first, first, second], axis=0)
    proj = jnp.einsum("ab,oc->aobc", half, proj_weight).reshape(6, 128)
    proj = jnp.concatenate([proj, jnp.zeros((10, 128), jnp.float32)], axis=0)
    proj = jnp.concatenate(split_terms(proj), axis=0)

    result = pl.pallas_call(
        rollout_kernel,
        out_shape=jax.ShapeDtypeStruct((STEPS, 16, 2048), jnp.float32),
        in_specs=[vmem] * 5,
        out_specs=vmem,
        scratch_shapes=[
            pltpu.VMEM((8, 16, 16, 128), jnp.float32),
            pltpu.VMEM((8, 16, 16, 128), jnp.float32),
            pltpu.VMEM((8, 24, 16, 128), jnp.bfloat16),
            pltpu.VMEM((768, 384), jnp.bfloat16),
            pltpu.VMEM((16, 2048), jnp.float32),
        ],
        compiler_params=pltpu.CompilerParams(vmem_limit_bytes=VMEM_BYTES),
    )(x, lift, proj, packed, biases)

    own = result[:, :6].astype(jnp.bfloat16).reshape(STEPS, 2, comps, 4, 2, y_cells, z_cells)
    own = lax.dynamic_index_in_dim(own, slab_id, 4, keepdims=False)
    own = own.transpose(0, 2, 1, 3, 4, 5).reshape(STEPS, comps, slab_rows, y_cells, segments, z_cells // segments)
    base = segment_id - slot

    def part_for(target):
        return lax.dynamic_index_in_dim(own, target, 4, keepdims=False)

    parts = [part_for(segment_id)]
    for shift in range(1, crop_count):
        pairs = [(s, s - s % crop_count + (s + shift) % crop_count) for s in range(segments)]
        parts.append(lax.ppermute(part_for(base + (slot + shift) % crop_count), "segment", pairs))
    parts = jnp.stack(parts)
    order = (slot - jnp.arange(crop_count)) % crop_count
    return jnp.take(parts, order, axis=0).transpose(1, 0, 2, 3, 4, 5).astype(jnp.float32)


def solution(mesh):
    in_specs = (
        P("groups", None, "slab", None, None),
        P("groups", None),
        P(),
        P("segment", None, None, None, None),
        P("segment", None, None),
        P(),
    )
    out_specs = P(None, "groups", None, "slab", None, "segment")
    return jax.shard_map(shards, mesh=mesh, in_specs=in_specs, out_specs=out_specs, check_vma=False)
```

time: 964 us -> 221 us (0.23)
  waiting for transfers between devices: 466 us -> 63.9 us
  other arithmetic: 152 us -> 3.43 us
  starting transfers between devices: 139 us -> 3.67 us
  matrix products: 105 us -> 0 us
  Pallas kernels: 0 us -> 101 us
  local copies, waits for them, and re-layouts: 76 us -> 7.04 us
  blocking collectives: 0 us -> 27.9 us
    ppermute x140 -> x4, waiting for transfers between devices: 405 us -> 2.16 us  [the longest x3 2.16 us: shards(): lax.ppermute(part_for(base + (slot + shift) % crop_count), 'segment', pairs)]
    ppermute x140 -> x4, starting transfers between devices: 139 us -> 3.67 us  [the longest x3 3.16 us: shards(): lax.ppermute(part_for(base + (slot + shift) % crop_count), 'segment', pairs)]
    dot_general x256 -> x0, matrix products: 105 us -> none  [the longest x216 57.1 us: dilated_conv(): jnp.einsum('oc,cxp->oxp', layer_weights[(tap_x + 1) * 3 + tap_y + 1], win...]
    pallas_call x0 -> x2, Pallas kernels: none -> 101 us  [the longest x1 99.7 us: shards(): pl.pallas_call(rollout_kernel, out_shape=jax.ShapeDtypeStruct((STEPS, 16,...]
    select_n x164 -> x1, other arithmetic: 62.9 us -> 0.01 us  [shards(): jnp.take(parts, order, axis=0).transpose(1, 0, 2, 3, 4, 5)]
    all_gather x0 -> x1, waiting for transfers between devices: none -> 61.7 us  [shards(): packed = lax.all_gather(packed, 'segment')]
    reduce_scatter x1 -> x0, waiting for transfers between devices: 61.2 us -> none  [shards(): lax.psum_scatter(shaped.astype(jnp.bfloat16), 'segment', scatter_dimensio...]
    slice x224 -> x4, local copies, waits for them, and re-layouts: 48.9 us -> 1.5 us  [the longest x1 0.76 us: shards(): lift_weight[:, :comps]]
  transfers between devices with their start and end apart: 141 -> 5, of which waited for: 141 -> 3; matrix products, arithmetic and copies ran while one was open for 0% -> 3% of each run, Pallas kernels for 0% -> 0%
where the time goes in v1:
time: 221 us
  Pallas kernels  101 us (46%)
  waiting for transfers between devices  63.9 us (29%)
  blocking collectives  27.9 us (13%)
  between operations  13.7 us (6%)
  local copies, waits for them, and re-layouts  7.04 us (3%)
  starting transfers between devices  3.67 us (2%)
  other arithmetic  3.43 us (2%)
    pallas_call x1, Pallas kernels, shards(): pl.pallas_call(rollout_kernel, out_shape=jax.ShapeDtypeStruct((STEPS, 16,...  99.7 us
    all_gather x1, waiting for transfers between devices, shards(): packed = lax.all_gather(packed, 'segment')  61.7 us
    all_gather x1, blocking collectives, shards(): biases = lax.all_gather(conv_bias[0], 'segment')  27.9 us
  transfers between devices with their start and end apart: 5, of which 3 were waited for; matrix products, arithmetic and copies ran while one was open for 3% of the time, Pallas kernels for 0%

profile of v1, /device:TPU:0, one launch (start us, length us, event | category | flops | bytes accessed | tf_op | source)
XLA Modules:
  0.0 220.8 jit_solution(6055541140944755121)
XLA Ops:
  6.6 1.2 copy-done.1
  7.8 1.4 shard_map.64
  9.3 0.5 collective-permute-start
  9.8 0.8 fusion.19
  10.7 0.1 reshape.98
  10.7 0.1 reshape.99
  10.8 0.8 multiply_bitcast_fusion
  11.6 0.1 reshape.100
  11.7 0.7 copy.27
  12.3 27.9 %all_gather.11 = f32[8,3,64]{2,1,0:T(4,128)S(1)} all-gather(f32[1,3,64]{2,1,0:T(4,128)S(1)} %copy.27), channel_id=1, replica_groups=mesh['groups'=2,'segment'=8,'slab'=2] {'segment'}, dimensions={0}, use_global_device_ids=true | all-gather | bytes 6912 | tf_op jit(solution)/shard_map/all_gather | solution.py:167
  40.3 0.1 pad.18.clone
  40.4 0.7 constant_dynamic-slice_fusion.4
  41.1 0.7 fusion.20
  41.7 1.3 fusion.10
  43.1 0.7 fusion.7
  44.0 0.1 stack_broadcast_in_dim.6
  44.3 0.2 reshape.97
  44.7 0.2 reshape.96
  44.9 0.1 maximum_maximum_fusion.x_ref
  45.0 61.7 %all-gather.3.cloned.1.call-done = bf16[24,960,128]{2,1,0:T(8,128)(2,1)} async-done(((bf16[3,960,128]{2,1,0:T(8,128)(2,1)}), bf16[24,960,128]{2,1,0:T(8,128)(2,1)}) %all-gather.3.cloned.1.call-update) | async-done | bytes 5898256 | tf_op jit(solution)/shard_map/all_gather | solution.py:166
  106.7 99.7 %shard_map.65 = f32[2,16,2048]{2,1,0:T(8,128)S(1)} custom-call(f32[16,2048]{1,0:T(8,128)S(1)} %maximum_maximum_fusion.x_ref, bf16[48,128]{1,0:T(8,128)(2,1)S(1)} %get-tuple-element.20.lift_ref, bf16[48,128]{1,0:T(8,128)(2,1)S(1)} %get-tuple-element.21.proj_ref, bf16[8,3,960,128]{3,2,1,0:T(8,128)(2,1)} %bitcast.52, f32[8,3,1,128]{3,2,1,0:T(1,128)S(1)} %copy.30.bias_ref), custom_call_target="tpu_custom_call" | custom-call | tf_op jit(solution)/shard_map/pallas_call | solution.py:197
  206.5 0.3 reshape.101
  206.9 0.1 copy.33
  207.0 0.1 constant_dynamic-slice_fusion.3
  207.1 0.6 collective-permute-start.1
  207.7 0.2 collective-permute-start.2
  207.9 2.4 %collective-permute-start.3 = (bf16[2,3,8,16,2]{3,2,4,1,0:T(8,128)(2,1)S(1)}, bf16[2,3,8,16,2]{3,2,4,1,0:T(8,128)(2,1)S(1)}, u32[]{:S(2)}, u32[]{:S(2)}) collective-permute-start(bf16[2,3,8,16,2]{3,2,4,1,0:T(8,128)(2,1)S(1)} %bitcast.62), channel_id=1, source_target_pairs={{0,6},{2,0},{4,2},{6,4},{8,14},{10,8},{12,10},{14,12},{1,7},{3,1},... | collective-permute-start | bytes 9224 | tf_op jit(solution)/shard_map/ppermute | solution.py:223
  210.3 1.6 collective-permute-done.1
  211.9 0.6 collective-permute-done.3
  212.5 0.6 gather_fusion
  213.1 0.1 convert_bitcast_fusion
  213.2 0.8 copy.38
  (37 shorter events, 0.8 us)
Async XLA Ops:
  6.5 2.7 %copy-start = (f32[4,3,8,16,16]{4,3,2,1,0:T(8,128)S(1)}, f32[4,3,8,16,16]{4,3,2,1,0:T(8,128)}, u32[]{:S(2)}) copy-start(f32[4,3,8,16,16]{4,3,2,1,0:T(8,128)} %param.6) | copy-start | bytes 294916
  6.5 100.2 %all-gather.3.cloned.1.call-start = ((), (), s32[]{:S(2)}) async-start(), calls=%async_computation | async-start | bytes 6635520 | tf_op jit(solution)/shard_map/all_gather | solution.py:166
  6.6 1.2 copy-start.1
  9.3 35.3 %collective-permute-start = (f32[3,8,16,16]{3,2,1,0:T(8,128)S(1)}, f32[3,8,16,16]{3,2,1,0:T(8,128)S(1)}, u32[]{:S(2)}, u32[]{:S(2)}) collective-permute-start(f32[3,8,16,16]{3,2,1,0:T(8,128)S(1)} %fusion.21), channel_id=1, source_target_pairs={{0,1},{1,0},{2,3},{3,2},{4,5},{5,4},{6,7},{7,6},{8,9},{9,8},{10,11... | collective-permute-start | bytes 73736 | tf_op jit(solution)/shard_map/ppermute | solution.py:171
  207.1 4.8 %collective-permute-start.1 = (bf16[2,3,8,16,2]{3,2,4,1,0:T(8,128)(2,1)S(1)}, bf16[2,3,8,16,2]{3,2,4,1,0:T(8,128)(2,1)S(1)}, u32[]{:S(2)}, u32[]{:S(2)}) collective-permute-start(bf16[2,3,8,16,2]{3,2,4,1,0:T(8,128)(2,1)S(1)} %bitcast.60), channel_id=1, source_target_pairs={{0,2},{2,4},{4,6},{6,0},{8,10},{10,12},{12,14},{14,8},{1,3},{3,5},... | collective-permute-start | bytes 9224 | tf_op jit(solution)/shard_map/ppermute | solution.py:223
  207.7 4.2 %collective-permute-start.2 = (bf16[2,3,8,16,2]{3,2,4,1,0:T(8,128)(2,1)S(1)}, bf16[2,3,8,16,2]{3,2,4,1,0:T(8,128)(2,1)S(1)}, u32[]{:S(2)}, u32[]{:S(2)}) collective-permute-start(bf16[2,3,8,16,2]{3,2,4,1,0:T(8,128)(2,1)S(1)} %bitcast.61), channel_id=1, source_target_pairs={{0,4},{2,6},{4,0},{6,2},{8,12},{10,14},{12,8},{14,10},{1,5},{3,7},... | collective-permute-start | bytes 9224 | tf_op jit(solution)/shard_map/ppermute | solution.py:223
  207.9 4.6 %collective-permute-start.3 = (bf16[2,3,8,16,2]{3,2,4,1,0:T(8,128)(2,1)S(1)}, bf16[2,3,8,16,2]{3,2,4,1,0:T(8,128)(2,1)S(1)}, u32[]{:S(2)}, u32[]{:S(2)}) collective-permute-start(bf16[2,3,8,16,2]{3,2,4,1,0:T(8,128)(2,1)S(1)} %bitcast.62), channel_id=1, source_target_pairs={{0,6},{2,0},{4,2},{6,4},{8,14},{10,8},{12,10},{14,12},{1,7},{3,1},... | collective-permute-start | bytes 9224 | tf_op jit(solution)/shard_map/ppermute | solution.py:223
Sparse Core Ops, SparseCore 0:
  9.5 97.1 all-gather.2
